TPU v7x, 32 devices: a whole 2x2x4 slice. The times are simulated.
32 devices in a mesh: seq: 16 (over z, y, x), geo: 2 (over core).
Axes of the slice: x: 2, y: 2, z: 4, core: 2. Of those that a mesh axis runs over, the one named last changes fastest.
Arguments:
- cells: bfloat16 [8192, 1024], P(('geo', 'seq')), parts along dimension 0, may hold values from -8 to 8
- anchor_index: int32 [256], P(('geo', 'seq')), parts along dimension 0, may hold values from 0 to 4095, as said below
- queries: bfloat16 [8192, 1024], P(('geo', 'seq')), parts along dimension 0, may hold values from -8 to 8
- norm_gain: float32 [1024], replicated, may hold values from 0.25 to 1.75
- w_qkv: bfloat16 [1024, 3072], P('seq'), may hold values from -1 to 1
- w_out: bfloat16 [1024, 1024], P('seq'), may hold values from -0.1875 to 0.1875
Outputs:
- anchor_out: bfloat16 [256, 1024], P(('geo', 'seq')), parts along dimension 0
- query_out: bfloat16 [8192, 1024], P(('geo', 'seq')), parts along dimension 0
There are 2 independent parts, one for each index of `geo`. A program takes and returns all parts, laid end to end along the dimension named above; an argument that names none is the same for every part. Nothing has to cross between parts.
Inputs may be any that keep to these rules, and one draw needn't show every extreme that they name: `anchor_index`: the 8 anchors of each seq block name cells of the same block of 256 cells; repeats may occur.
All inputs are finite; a program needn't handle non-finite values.
Results may differ from a plain program's by a relative error of at most 0.0091.
Values may be sent and summed in bfloat16 or wider, within the bound.
A program may use at most 64 MiB of HBM per device.

v0:
```python
import jax
import jax.numpy as jnp
from jax import lax
from jax.sharding import PartitionSpec as P

HEADS = 16


def normalize(rows, norm_gain):
    values = rows.astype(jnp.float32)
    scale = lax.rsqrt(jnp.mean(values * values, axis=-1, keepdims=True) + 1e-05)
    return (values * scale * norm_gain).astype(jnp.bfloat16)


def split_heads(rows, heads):
    return rows.reshape(rows.shape[0], heads, rows.shape[1] // heads).transpose(1, 0, 2)


def attend_whole(query_rows, key_rows, value_rows, heads):
    count, width = query_rows.shape
    factor = (width // heads) ** (-0.5)

    def single(items):
        qpart, kpart, vpart = items
        scores = jnp.dot(qpart, kpart.T, preferred_element_type=jnp.float32) * factor
        peak = jnp.max(scores, axis=-1, keepdims=True)
        expo = jnp.exp(scores - peak)
        total = jnp.sum(expo, axis=-1, keepdims=True)
        mixed = jnp.dot(expo.astype(jnp.bfloat16), vpart, preferred_element_type=jnp.float32)
        return (mixed / total).astype(jnp.bfloat16)

    result = lax.map(
        single,
        (
            split_heads(query_rows, heads),
            split_heads(key_rows, heads),
            split_heads(value_rows, heads),
        ),
    )
    return result.transpose(1, 0, 2).reshape(count, width)


def local(cells, anchor_index, queries, norm_gain, w_qkv, w_out):
    heads = HEADS
    width = cells.shape[1]
    anchor_rows = anchor_index.shape[0]
    local_index = anchor_index - lax.axis_index("seq") * cells.shape[0]
    anchors = jnp.take(cells, local_index, axis=0)
    norm_a = normalize(anchors, norm_gain)
    norm_q = normalize(queries, norm_gain)
    piece = lax.all_gather(w_qkv, "seq", axis=0, tiled=True)
    total_a = jnp.dot(norm_a, piece, preferred_element_type=jnp.float32)
    total_q = jnp.dot(norm_q, piece[:, :width], preferred_element_type=jnp.float32)
    qkv_a = total_a.astype(jnp.bfloat16)
    q_q = total_q.astype(jnp.bfloat16)
    k_a = qkv_a[:, width : 2 * width]
    v_a = qkv_a[:, 2 * width :]
    all_query = jnp.concatenate([qkv_a[:, :width], q_q], axis=0)
    keys_all, values_all = (
        lax.all_gather(k_a, "seq", axis=0, tiled=True),
        lax.all_gather(v_a, "seq", axis=0, tiled=True),
    )
    context = attend_whole(all_query, keys_all, values_all, heads)
    projected = jnp.dot(
        context,
        lax.all_gather(w_out, "seq", axis=0, tiled=True),
        preferred_element_type=jnp.float32,
    )
    projected = projected.astype(jnp.bfloat16)
    return (projected[:anchor_rows], projected[anchor_rows:])


def solution(mesh):
    placed = (
        P(("geo", "seq"), None),
        P(("geo", "seq")),
        P(("geo", "seq"), None),
        P(),
        P("seq", None),
        P("seq", None),
    )
    return jax.shard_map(
        local,
        mesh=mesh,
        in_specs=placed,
        out_specs=(P(("geo", "seq"), None), P(("geo", "seq"), None)),
        check_vma=False,
    )
```

profile of v0, /device:TPU:0, one launch (start us, length us, event | category | flops | bytes accessed | tf_op | source)
XLA Modules:
  0.0 215.9 jit_solution(716176549606692596)
XLA Ops:
  7.2 0.7 all-gather.3.cloned.1.call-update
  8.0 0.7 all-gather.5.cloned.1.call-update
  8.7 0.7 compare_and_fusion
  9.4 0.6 gather_fusion
  10.1 1.2 fusion.20
  11.4 96.3 %all-gather.3.cloned.1.call-done = bf16[1024,3072]{1,0:T(8,128)(2,1)} async-done(((bf16[64,3072]{1,0:T(8,128)(2,1)}), bf16[1024,3072]{1,0:T(8,128)(2,1)}) %all-gather.3.cloned.1.call-update) | async-done | bytes 6291472 | tf_op jit(solution)/shard_map/all_gather | solution.py:51
  107.7 3.8 %convolution_convert_fusion = bf16[8,3072]{1,0:T(8,128)(2,1)S(1)} fusion(bf16[1024,3072]{1,0:T(8,128)(2,1)} %all-gather.3.cloned.1.call-done, f32[1024]{0:T(1024)} %param.11, f32[8]{0:T(128)S(1)} %add_rsqrt_fusion.1, bf16[8,1024]{1,0:T(8,128)(2,1)S(1)} %gather_fusion, pred[8]{0:T(512)(128)(4,1)S(1)} %get-tuple-element.45), kind=kOutput, calls=%fused_computation.18 | convolution fusion | flops 50397184 | bytes 6361128 | tf_op jit(solution)/shard_map/dot_general | solution.py:52
  111.4 2.4 %fusion.17 = bf16[256,1024]{1,0:T(8,128)(2,1)S(1)} fusion(bf16[1024,3072]{1,0:T(8,128)(2,1)} %all-gather.3.cloned.1.call-done, bf16[256,1024]{1,0:T(8,128)(2,1)S(1)} %copy-done.1, f32[1024]{0:T(1024)S(1)} %copy-done.2, f32[256]{0:T(256)S(1)} %add_rsqrt_fusion), kind=kOutput, calls=%fused_computation.24 | convolution fusion | flops 538181632 | bytes 3150848 | tf_op jit(solution)/shard_map/dot_general | solution.py:53
  113.9 0.4 copy.11
  114.2 39.9 %all_gather.13 = bf16[128,1024]{1,0:T(8,128)(2,1)S(1)} all-gather(bf16[8,1024]{1,0:T(8,128)(2,1)S(1)} %get-tuple-element.50), channel_id=1, replica_groups=mesh['seq'=16,'geo'=2] {'seq'}, dimensions={0}, use_global_device_ids=true | all-gather | bytes 278528 | tf_op jit(solution)/shard_map/all_gather | solution.py:60
  154.3 37.5 %all_gather.14 = bf16[128,1024]{1,0:T(8,128)(2,1)S(1)} all-gather(bf16[8,1024]{1,0:T(8,128)(2,1)S(1)} %get-tuple-element.49), channel_id=1, replica_groups=mesh['seq'=16,'geo'=2] {'seq'}, dimensions={0}, use_global_device_ids=true | all-gather | bytes 278528 | tf_op jit(solution)/shard_map/all_gather | solution.py:61
  192.0 13.2 %while.10 = (s32[]{:T(128)}, bf16[16,264,64]{1,2,0:T(8,128)(2,1)S(1)}, bf16[16,264,64]{1,2,0:T(8,128)(2,1)S(1)}, bf16[16,128,64]{1,2,0:T(8,128)(2,1)S(1)}, bf16[16,128,64]{1,2,0:T(8,128)(2,1)S(1)}, /*index=5*/s32[]{:T(128)}) while((s32[]{:T(128)}, bf16[16,264,64]{1,2,0:T(8,128)(2,1)S(1)}, bf16[16,264,64]{1,2,0:T(8,128)(2,1)S(1)}, ...), condition=%wide.region_5.6_spmd, body=%wide.region_2.0_spmd.sunk | while | flops 8886770 | bytes 545957 | solution.py:32
  192.0 0.3 fusion.45
  192.6 0.3 fusion.47
  192.9 0.3 fusion.45
  193.7 0.3 fusion.45
  194.5 0.3 fusion.45
  195.3 0.3 fusion.45
  196.2 0.3 fusion.45
  197.0 0.3 fusion.45
  197.8 0.3 fusion.45
  198.6 0.3 fusion.45
  199.5 0.3 fusion.45
  200.3 0.3 fusion.45
  201.1 0.3 fusion.45
  201.9 0.3 fusion.45
  202.8 0.3 fusion.45
  203.6 0.3 fusion.45
  204.4 0.3 fusion.45
  205.3 2.3 %convolution_convert_fusion.1 = bf16[264,1024]{1,0:T(8,128)(2,1)S(1)} fusion(bf16[264,1024]{0,1:T(8,128)(2,1)S(1)} %bitcast.44, bf16[1024,1024]{1,0:T(8,128)(2,1)} %all-gather.5.cloned.1.call-done), kind=kOutput, calls=%fused_computation.23 | convolution fusion | flops 553918464 | bytes 3178496 | tf_op jit(solution)/shard_map/dot_general | solution.py:64
  207.6 0.8 slice.31
  208.5 0.6 slice.30
  (49 shorter events, 8.2 us)
Async XLA Ops:
  7.2 2.2 %copy-start = (bf16[256,1024]{1,0:T(8,128)(2,1)S(1)}, bf16[256,1024]{1,0:T(8,128)(2,1)}, u32[]{:S(2)}) copy-start(bf16[256,1024]{1,0:T(8,128)(2,1)} %param.8) | copy-start | bytes 1572868
  7.2 100.5 %all-gather.3.cloned.1.call-start = ((), (), s32[]{:S(2)}) async-start(), calls=%async_computation | async-start | bytes 6684672 | tf_op jit(solution)/shard_map/all_gather | solution.py:51
  7.9 197.4 %all-gather.5.cloned.1.call-start = ((), (), s32[]{:S(2)}) async-start(), calls=%async_computation.1 | async-start | bytes 2228224 | tf_op jit(solution)/shard_map/all_gather | solution.py:66
  11.4 100.0 %copy-start.1 = (bf16[256,1024]{1,0:T(8,128)(2,1)S(1)}, bf16[256,1024]{1,0:T(8,128)(2,1)}, u32[]{:S(2)}) copy-start(bf16[256,1024]{1,0:T(8,128)(2,1)} %param.10) | copy-start | bytes 1572868
  11.4 100.0 %copy-start.2 = (f32[1024]{0:T(1024)S(1)}, f32[1024]{0:T(1024)}, u32[]{:S(2)}) copy-start(f32[1024]{0:T(1024)} %param.11) | copy-start | bytes 12292
Sparse Core Ops, SparseCore 0:
  10.8 96.8 all-gather.2
  110.4 61.1 all-gather.4
where the time goes:
time: 216 us
  waiting for transfers between devices  97.7 us (45%)
  blocking collectives  77.5 us (36%)
  matrix products  17.7 us (8%)
  between operations  14.2 us (7%)
  other arithmetic  5.83 us (3%)
  local copies, waits for them, and re-layouts  2.73 us (1%)
    all_gather x1, waiting for transfers between devices, local(): piece = lax.all_gather(w_qkv, 'seq', axis=0, tiled=True)  96.3 us
    all_gather x1, blocking collectives, local(): lax.all_gather(k_a, 'seq', axis=0, tiled=True)  39.9 us
    all_gather x1, blocking collectives, local(): lax.all_gather(v_a, 'seq', axis=0, tiled=True)  37.5 us
    dot_general x16, matrix products, single(): jnp.dot(qpart, kpart.T, preferred_element_type=jnp.float32) * factor  5.18 us
  transfers between devices with their start and end apart: 2, of which 1 were waited for; matrix products, arithmetic and copies ran while one was open for 10% of the time, Pallas kernels for 0%

commit v1 on v0

--- a/solution.py
+++ b/solution.py
@@ -1,9 +1,16 @@
+import functools
+
 import jax
 import jax.numpy as jnp
 from jax import lax
+from jax.experimental import pallas as pl
+from jax.experimental.pallas import tpu as pltpu
 from jax.sharding import PartitionSpec as P
 
 HEADS = 16
+PLANE = 4
+LANES = 128
+MESH = pl.DeviceIdType.MESH
 
 
 def normalize(rows, norm_gain):
@@ -40,7 +47,7 @@
     return result.transpose(1, 0, 2).reshape(count, width)
 
 
-def local(cells, anchor_index, queries, norm_gain, w_qkv, w_out):
+def gathered(cells, anchor_index, queries, norm_gain, w_qkv, w_out):
     heads = HEADS
     width = cells.shape[1]
     anchor_rows = anchor_index.shape[0]
@@ -53,14 +60,9 @@
     total_q = jnp.dot(norm_q, piece[:, :width], preferred_element_type=jnp.float32)
     qkv_a = total_a.astype(jnp.bfloat16)
     q_q = total_q.astype(jnp.bfloat16)
-    k_a = qkv_a[:, width : 2 * width]
-    v_a = qkv_a[:, 2 * width :]
     all_query = jnp.concatenate([qkv_a[:, :width], q_q], axis=0)
-    keys_all, values_all = (
-        lax.all_gather(k_a, "seq", axis=0, tiled=True),
-        lax.all_gather(v_a, "seq", axis=0, tiled=True),
-    )
-    context = attend_whole(all_query, keys_all, values_all, heads)
+    keys_values = lax.all_gather(qkv_a[:, width:], "seq", axis=0, tiled=True)
+    context = attend_whole(all_query, keys_values[:, :width], keys_values[:, width:], heads)
     projected = jnp.dot(
         context,
         lax.all_gather(w_out, "seq", axis=0, tiled=True),
@@ -70,7 +72,318 @@
     return (projected[:anchor_rows], projected[anchor_rows:])
 
 
+def kernel(
+    lines,
+    index_ref,
+    cells_ref,
+    queries_ref,
+    gain_ref,
+    w_qkv_ref,
+    w_out_ref,
+    anchor_out_ref,
+    query_out_ref,
+    norm_ref,
+    q_ref,
+    ctx_ref,
+    na_all,
+    wkv,
+    kv_all,
+    wq_all,
+    wo_all,
+    send_sem,
+    na_sem,
+    a2a_sem,
+    kv_sem,
+    wq_sem,
+    wo_sem,
+    wq_sib_sem,
+    wo_sib_sem,
+):
+    count = lines * PLANE
+    me = lax.axis_index("seq")
+    core = lax.axis_index("geo")
+    line = me // PLANE
+    spot = me % PLANE
+    width = cells_ref.shape[1]
+    half = width // 2
+    mine = pl.ds(pl.multiple_of(core * half, LANES), half)
+    other = pl.ds(pl.multiple_of((1 - core) * half, LANES), half)
+    anchors = index_ref.shape[0]
+    rows = queries_ref.shape[0]
+
+    barrier = pltpu.get_barrier_semaphore()
+    for k in range(1, count):
+        pl.semaphore_signal(
+            barrier, inc=1, device_id={"seq": (me + k) % count}, device_id_type=MESH
+        )
+    pl.semaphore_signal(barrier, inc=1, device_id={"geo": 1 - core}, device_id_type=MESH)
+
+    started = []
+
+    def send(src, dst, sem, target):
+        copy = pltpu.make_async_remote_copy(
+            src_ref=src,
+            dst_ref=dst,
+            send_sem=send_sem.at[len(started)],
+            recv_sem=sem,
+            device_id=target,
+            device_id_type=MESH,
+        )
+        copy.start()
+        started.append(copy)
+
+    def arrived(dst, sem):
+        pltpu.make_async_remote_copy(
+            src_ref=dst,
+            dst_ref=dst,
+            send_sem=send_sem.at[0],
+            recv_sem=sem,
+            device_id={"geo": 1 - core},
+            device_id_type=MESH,
+        ).wait_recv()
+
+    gain = gain_ref[...]
+
+    row = lax.broadcasted_iota(jnp.int32, (anchors, cells_ref.shape[0]), 0)
+    column = lax.broadcasted_iota(jnp.int32, (anchors, cells_ref.shape[0]), 1)
+    wanted = jnp.zeros_like(row)
+    for a in range(anchors):
+        wanted = jnp.where(row == a, index_ref[a] - me * cells_ref.shape[0], wanted)
+    pick = jnp.where(wanted == column, 1.0, 0.0).astype(jnp.bfloat16)
+    picked = jnp.dot(pick, cells_ref[...], preferred_element_type=jnp.float32)
+    scale = lax.rsqrt(jnp.mean(picked * picked, axis=-1, keepdims=True) + 1e-05)
+    norm_a = picked * scale * gain
+    na_all[line, spot] = jnp.concatenate([norm_a[:, :half], norm_a[:, half:]], axis=0).astype(
+        jnp.bfloat16
+    )
+    norm_ref[pl.ds(rows, 2 * anchors), :] = jnp.concatenate([norm_a, norm_a], axis=0).astype(
+        jnp.bfloat16
+    )
+    wq_all[line, spot] = w_qkv_ref[:, :width]
+    wo_all[line, spot] = w_out_ref[...]
+    wkv[me] = w_qkv_ref[:, pl.ds(pl.multiple_of(width + me * LANES, LANES), LANES)]
+
+    pl.semaphore_wait(barrier, count)
+
+    def on_line(k):
+        return (line + k) % lines
+
+    def on_plane(k):
+        return (spot + k) % PLANE
+
+    def line_target(k):
+        return {"seq": on_line(k) * PLANE + spot}
+
+    def plane_target(k):
+        return {"seq": line * PLANE + on_plane(k)}
+
+    sibling = {"geo": 1 - core}
+
+    for k in range(1, lines):
+        block = na_all.at[line, spot]
+        send(block, block, na_sem.at[line], line_target(k))
+    for k in range(1, count):
+        to = (me + k) % count
+        start = pl.multiple_of(width + to * LANES, LANES)
+        send(w_qkv_ref.at[:, pl.ds(start, LANES)], wkv.at[me], a2a_sem.at[me], {"seq": to})
+
+    def to_line(whole, sem):
+        block = whole.at[line, spot, :, mine]
+        for k in range(1, lines):
+            send(block, block, sem.at[line, spot], line_target(k))
+
+    def to_plane(whole, sem, at):
+        block = whole.at[at, spot, :, mine]
+        for k in range(1, PLANE):
+            send(block, block, sem.at[at, spot], plane_target(k))
+
+    def to_sibling(whole, sem, at, where):
+        block = whole.at[at, where, :, mine]
+        send(block, block, sem.at[at, where], sibling)
+
+    to_line(wq_all, wq_sem)
+    to_plane(wq_all, wq_sem, line)
+    to_line(wo_all, wo_sem)
+
+    values = queries_ref[...].astype(jnp.float32)
+    scale = lax.rsqrt(jnp.mean(values * values, axis=-1, keepdims=True) + 1e-05)
+    norm_ref[pl.ds(0, rows), :] = (values * scale * gain).astype(jnp.bfloat16)
+
+    for k in range(1, lines):
+        arrived(na_all.at[on_line(k), spot], na_sem.at[on_line(k)])
+    for k in range(1, PLANE):
+        block = na_all.at[:, spot]
+        send(block, block, na_sem.at[lines + spot], plane_target(k))
+    for k in range(1, lines):
+        at = on_line(k)
+        arrived(wq_all.at[at, spot, :, mine], wq_sem.at[at, spot])
+        to_plane(wq_all, wq_sem, at)
+        to_sibling(wq_all, wq_sib_sem, at, spot)
+
+    for k in range(1, PLANE):
+        arrived(na_all.at[:, on_plane(k)], na_sem.at[lines + on_plane(k)])
+    for k in range(1, count):
+        source = (me + k) % count
+        arrived(wkv.at[source], a2a_sem.at[source])
+    packed = na_all[...].reshape(count * 2 * anchors, half)
+    slab = wkv[...].reshape(width, LANES)
+    low = jnp.dot(packed, slab[:half], preferred_element_type=jnp.float32)
+    high = jnp.dot(packed, slab[half:], preferred_element_type=jnp.float32)
+    low = low.reshape(count, 2 * anchors, LANES)[:, :anchors]
+    high = high.reshape(count, 2 * anchors, LANES)[:, anchors:]
+    kv_all[line, spot] = (low + high).reshape(count * anchors, LANES).astype(jnp.bfloat16)
+
+    for k in range(1, lines):
+        block = kv_all.at[line, spot]
+        send(block, block, kv_sem.at[line], line_target(k))
+    to_plane(wo_all, wo_sem, line)
+    for k in range(1, lines):
+        arrived(kv_all.at[on_line(k), spot], kv_sem.at[on_line(k)])
+    for k in range(1, PLANE):
+        block = kv_all.at[:, spot]
+        send(block, block, kv_sem.at[lines + spot], plane_target(k))
+    for k in range(1, lines):
+        at = on_line(k)
+        arrived(wo_all.at[at, spot, :, mine], wo_sem.at[at, spot])
+        to_plane(wo_all, wo_sem, at)
+        to_sibling(wo_all, wo_sib_sem, at, spot)
+
+    def rest_to_sibling(whole, sem, sib_sem):
+        for j in range(lines):
+            for k in range(1, PLANE):
+                at, where = on_line(j), on_plane(k)
+                arrived(whole.at[at, where, :, mine], sem.at[at, where])
+                to_sibling(whole, sib_sem, at, where)
+
+    def from_sibling(whole, sib_sem):
+        for j in range(lines):
+            for k in range(PLANE):
+                if j or k:
+                    at, where = on_line(j), on_plane(k)
+                    arrived(whole.at[at, where, :, other], sib_sem.at[at, where])
+
+    rest_to_sibling(wq_all, wq_sem, wq_sib_sem)
+    from_sibling(wq_all, wq_sib_sem)
+    step = 2 * LANES
+    for j in range(width // step):
+        columns = pl.ds(j * step, step)
+        block = wq_all[:, :, :, columns].reshape(width, step)
+        q_ref[:, columns] = jnp.dot(
+            norm_ref[...], block, preferred_element_type=jnp.float32
+        ).astype(jnp.bfloat16)
+
+    for k in range(1, PLANE):
+        arrived(kv_all.at[:, on_plane(k)], kv_sem.at[lines + on_plane(k)])
+
+    head = width // HEADS
+    factor = head ** (-0.5)
+    keys = count * anchors
+    upper = lax.broadcasted_iota(jnp.int32, (keys, LANES), 1) >= head
+    upper_ctx = lax.broadcasted_iota(jnp.int32, (norm_ref.shape[0], LANES), 1) >= head
+
+    def blocks(pair):
+        block = kv_all[pair // PLANE, pair % PLANE]
+        zero = jnp.zeros_like(block)
+        return jnp.concatenate([jnp.where(upper, zero, block), jnp.where(upper, block, zero)], axis=0)
+
+    pairs = HEADS // 2
+    for pair in range(pairs):
+        columns = pl.ds(pair * LANES, LANES)
+        scores = lax.dot_general(
+            q_ref[:, columns],
+            blocks(pair),
+            (((1,), (1,)), ((), ())),
+            preferred_element_type=jnp.float32,
+        )
+        scores = scores * factor
+        expos, totals = [], []
+        for side in range(2):
+            part = scores[:, side * keys : (side + 1) * keys]
+            expo = jnp.exp(part - jnp.max(part, axis=-1, keepdims=True))
+            totals.append(jnp.sum(expo, axis=-1, keepdims=True))
+            expos.append(expo.astype(jnp.bfloat16))
+        mixed = jnp.dot(
+            jnp.concatenate(expos, axis=1), blocks(pairs + pair), preferred_element_type=jnp.float32
+        )
+        total = jnp.where(upper_ctx, totals[1], totals[0])
+        ctx_ref[:, columns] = (mixed / total).astype(jnp.bfloat16)
+
+    rest_to_sibling(wo_all, wo_sem, wo_sib_sem)
+    from_sibling(wo_all, wo_sib_sem)
+    for j in range(width // step):
+        columns = pl.ds(j * step, step)
+        block = wo_all[:, :, :, columns].reshape(width, step)
+        result = jnp.dot(ctx_ref[...], block, preferred_element_type=jnp.float32)
+        query_out_ref[:, columns] = result[:rows].astype(jnp.bfloat16)
+        anchor_out_ref[:, columns] = result[rows : rows + anchors].astype(jnp.bfloat16)
+
+    for copy in started:
+        copy.wait_send()
+
+
+def fused(lines, cells, anchor_index, queries, norm_gain, w_qkv, w_out):
+    rows, width = queries.shape
+    anchors = anchor_index.shape[0]
+    depth = w_out.shape[0]
+    count = lines * PLANE
+    padded = rows + 2 * anchors
+    vmem = pl.BlockSpec(memory_space=pltpu.VMEM)
+    grid = (lines, PLANE)
+    bf16 = jnp.bfloat16
+    copies = 2 * (lines - 1 + PLANE - 1) + count - 1
+    copies += 2 * (lines - 1 + lines * (PLANE - 1) + count - 1)
+    return pl.pallas_call(
+        functools.partial(kernel, lines),
+        out_shape=(
+            jax.ShapeDtypeStruct((anchors, width), bf16),
+            jax.ShapeDtypeStruct((rows, width), bf16),
+        ),
+        in_specs=[pl.BlockSpec(memory_space=pltpu.SMEM)] + [vmem] * 5,
+        out_specs=(vmem, vmem),
+        scratch_shapes=[
+            pltpu.VMEM((padded, width), bf16),
+            pltpu.VMEM((padded, width), bf16),
+            pltpu.VMEM((padded, width), bf16),
+            pltpu.VMEM((*grid, 2 * anchors, width // 2), bf16),
+            pltpu.VMEM((count, depth, LANES), bf16),
+            pltpu.VMEM((*grid, count * anchors, LANES), bf16),
+            pltpu.VMEM((*grid, depth, width), bf16),
+            pltpu.VMEM((*grid, depth, width), bf16),
+            pltpu.SemaphoreType.DMA((copies,)),
+            pltpu.SemaphoreType.DMA((lines + PLANE,)),
+            pltpu.SemaphoreType.DMA((count,)),
+            pltpu.SemaphoreType.DMA((lines + PLANE,)),
+            pltpu.SemaphoreType.DMA(grid),
+            pltpu.SemaphoreType.DMA(grid),
+            pltpu.SemaphoreType.DMA(grid),
+            pltpu.SemaphoreType.DMA(grid),
+        ],
+        compiler_params=pltpu.CompilerParams(
+            collective_id=0, has_side_effects=True, vmem_limit_bytes=40 * 1024 * 1024
+        ),
+        cost_estimate=pl.CostEstimate(
+            flops=4 * padded * width * width, bytes_accessed=4 * width * width, transcendentals=0
+        ),
+    )(anchor_index, cells, queries, norm_gain.reshape(1, -1), w_qkv, w_out)
+
+
 def solution(mesh):
+    count, parts = mesh.shape["seq"], mesh.shape["geo"]
+
+    def local(cells, anchor_index, queries, norm_gain, w_qkv, w_out):
+        width = cells.shape[1]
+        args = (cells, anchor_index, queries, norm_gain, w_qkv, w_out)
+        tiles = (
+            parts == 2
+            and count % PLANE == 0
+            and count * LANES == 2 * width
+            and HEADS * LANES == 2 * width
+            and count * anchor_index.shape[0] == LANES
+        )
+        if tiles:
+            return fused(count // PLANE, *args)
+        return gathered(*args)
+
     placed = (
         P(("geo", "seq"), None),
         P(("geo", "seq")),

time: 216 us -> 59.9 us (0.28)
  the two profiles are of different devices: /device:TPU:0 before, /device:TPU:9 now
where the time goes in v1:
time: 59.9 us; the launch traced here: 59.6 us
  Pallas kernels  52.2 us (87%)
  local copies, waits for them, and re-layouts  6.72 us (11%)
  between operations  0.65 us (1%)
    pallas_call x1, Pallas kernels, fused(): pl.pallas_call(functools.partial(kernel, lines), out_shape=(jax.ShapeDtyp...  52.2 us
    unnamed x14, local copies, waits for them, and re-layouts  6.72 us

profile of v1, /device:TPU:9, one launch (start us, length us, event | category | flops | bytes accessed | tf_op | source)
XLA Modules:
  0.0 59.6 jit_solution(3017698196091169617)
XLA Ops:
  0.6 0.0 copy-start.5
  0.6 0.6 %copy-done.5 = s32[8]{0:T(128)S(1)} copy-done((s32[8]{0:T(128)S(1)}, s32[8]{0:T(128)}, u32[]{:S(2)}) %copy-start.5) | copy-done | bytes 56
  1.3 0.0 copy-start
  1.3 1.0 %copy-done = bf16[256,1024]{1,0:T(8,128)(2,1)S(1)} copy-done((bf16[256,1024]{1,0:T(8,128)(2,1)S(1)}, bf16[256,1024]{1,0:T(8,128)(2,1)}, u32[]{:S(2)}) %copy-start) | copy-done | bytes 524312
  2.3 0.0 copy-start.1
  2.3 1.0 %copy-done.1 = bf16[256,1024]{1,0:T(8,128)(2,1)S(1)} copy-done((bf16[256,1024]{1,0:T(8,128)(2,1)S(1)}, bf16[256,1024]{1,0:T(8,128)(2,1)}, u32[]{:S(2)}) %copy-start.1) | copy-done | bytes 524312
  3.4 0.0 copy-start.2
  3.4 1.0 %copy-done.2 = bf16[64,3072]{1,0:T(8,128)(2,1)S(1)} copy-done((bf16[64,3072]{1,0:T(8,128)(2,1)S(1)}, bf16[64,3072]{1,0:T(8,128)(2,1)}, u32[]{:S(2)}) %copy-start.2) | copy-done | bytes 393240
  4.4 0.0 copy-start.3
  4.4 0.9 %copy-done.3 = bf16[64,1024]{1,0:T(8,128)(2,1)S(1)} copy-done((bf16[64,1024]{1,0:T(8,128)(2,1)S(1)}, bf16[64,1024]{1,0:T(8,128)(2,1)}, u32[]{:S(2)}) %copy-start.3) | copy-done | bytes 131096
  5.3 0.0 copy-start.4
  5.3 0.7 %copy-done.4 = f32[1024]{0:T(1024)S(1)} copy-done((f32[1024]{0:T(1024)S(1)}, f32[1024]{0:T(1024)}, u32[]{:S(2)}) %copy-start.4) | copy-done | bytes 4120
  6.0 52.2 %shard_map.77 = (bf16[8,1024]{1,0:T(8,128)(2,1)S(1)}, bf16[256,1024]{1,0:T(8,128)(2,1)S(1)}) custom-call(s32[8]{0:T(128)S(1)} %copy-done.5, bf16[256,1024]{1,0:T(8,128)(2,1)S(1)} %copy-done, bf16[256,1024]{1,0:T(8,128)(2,1)S(1)} %copy-done.1, f32[1,1024]{1,0:T(1,128)S(1)} %bitcast.1, bf16[64,3072]{1,0:T(8,128)(2,1)S(1)} %copy-done.2, ...), custom_call_target="tpu_custom_call" | custom-call | flops 1140850688 | bytes 4194304 | tf_op jit(solution)/shard_map/pallas_call | solution.py:335
  58.2 0.6 %copy.10 = bf16[8,1024]{1,0:T(8,128)(2,1)} copy(bf16[8,1024]{1,0:T(8,128)(2,1)S(1)} %get-tuple-element.4) | data formatting | bytes 32768
  58.8 0.8 %copy.11 = bf16[256,1024]{1,0:T(8,128)(2,1)} copy(bf16[256,1024]{1,0:T(8,128)(2,1)S(1)} %get-tuple-element.5) | data formatting | bytes 1048576
Async XLA Ops:
  0.6 0.7 %copy-start.5 = (s32[8]{0:T(128)S(1)}, s32[8]{0:T(128)}, u32[]{:S(2)}) copy-start(s32[8]{0:T(128)} %index_ref.1) | copy-start | bytes 100
  1.3 1.0 %copy-start = (bf16[256,1024]{1,0:T(8,128)(2,1)S(1)}, bf16[256,1024]{1,0:T(8,128)(2,1)}, u32[]{:S(2)}) copy-start(bf16[256,1024]{1,0:T(8,128)(2,1)} %cells_ref.1) | copy-start | bytes 1572868
  2.3 1.0 %copy-start.1 = (bf16[256,1024]{1,0:T(8,128)(2,1)S(1)}, bf16[256,1024]{1,0:T(8,128)(2,1)}, u32[]{:S(2)}) copy-start(bf16[256,1024]{1,0:T(8,128)(2,1)} %queries_ref.1) | copy-start | bytes 1572868
  3.4 1.0 %copy-start.2 = (bf16[64,3072]{1,0:T(8,128)(2,1)S(1)}, bf16[64,3072]{1,0:T(8,128)(2,1)}, u32[]{:S(2)}) copy-start(bf16[64,3072]{1,0:T(8,128)(2,1)} %w_qkv_ref.1) | copy-start | bytes 1179652
  4.4 0.9 %copy-start.3 = (bf16[64,1024]{1,0:T(8,128)(2,1)S(1)}, bf16[64,1024]{1,0:T(8,128)(2,1)}, u32[]{:S(2)}) copy-start(bf16[64,1024]{1,0:T(8,128)(2,1)} %w_out_ref.1) | copy-start | bytes 393220
  5.3 0.7 %copy-start.4 = (f32[1024]{0:T(1024)S(1)}, f32[1024]{0:T(1024)}, u32[]{:S(2)}) copy-start(f32[1024]{0:T(1024)} %param.9) | copy-start | bytes 12292

commit v2 on v1

--- a/solution.py
+++ b/solution.py
@@ -75,13 +75,16 @@
 def kernel(
     lines,
     index_ref,
-    cells_ref,
-    queries_ref,
-    gain_ref,
+    cells_hbm,
+    queries_hbm,
+    gain_hbm,
     w_qkv_ref,
     w_out_ref,
     anchor_out_ref,
     query_out_ref,
+    cells_ref,
+    queries_ref,
+    gain_ref,
     norm_ref,
     q_ref,
     ctx_ref,
@@ -90,6 +93,7 @@
     kv_all,
     wq_all,
     wo_all,
+    load_sem,
     send_sem,
     na_sem,
     a2a_sem,
@@ -111,12 +115,32 @@
     anchors = index_ref.shape[0]
     rows = queries_ref.shape[0]
 
+    flip_x = 1 - 2 * (spot % 2)
+    flip_y = 2 - 4 * (spot // 2)
+    near = spot + flip_x * (1 - core) + flip_y * core
+    far = spot + flip_y * (1 - core) + flip_x * core
+    cross = spot + flip_x + flip_y
+
     barrier = pltpu.get_barrier_semaphore()
     for k in range(1, count):
         pl.semaphore_signal(
             barrier, inc=1, device_id={"seq": (me + k) % count}, device_id_type=MESH
         )
     pl.semaphore_signal(barrier, inc=1, device_id={"geo": 1 - core}, device_id_type=MESH)
+
+    start = pl.multiple_of(width + me * LANES, LANES)
+    loads = []
+    for source, target in (
+        (cells_hbm, cells_ref),
+        (gain_hbm, gain_ref),
+        (w_qkv_ref.at[:, pl.ds(0, width)], wq_all.at[line, spot]),
+        (w_qkv_ref.at[:, pl.ds(start, LANES)], wkv.at[me]),
+        (w_out_ref, wo_all.at[line, spot]),
+        (queries_hbm, queries_ref),
+    ):
+        load = pltpu.make_async_copy(source, target, load_sem.at[len(loads)])
+        load.start()
+        loads.append(load)
 
     started = []
 
@@ -142,6 +166,8 @@
             device_id_type=MESH,
         ).wait_recv()
 
+    loads[0].wait()
+    loads[1].wait()
     gain = gain_ref[...]
 
     row = lax.broadcasted_iota(jnp.int32, (anchors, cells_ref.shape[0]), 0)
@@ -159,9 +185,8 @@
     norm_ref[pl.ds(rows, 2 * anchors), :] = jnp.concatenate([norm_a, norm_a], axis=0).astype(
         jnp.bfloat16
     )
-    wq_all[line, spot] = w_qkv_ref[:, :width]
-    wo_all[line, spot] = w_out_ref[...]
-    wkv[me] = w_qkv_ref[:, pl.ds(pl.multiple_of(width + me * LANES, LANES), LANES)]
+    for load in loads[2:5]:
+        load.wait()
 
     pl.semaphore_wait(barrier, count)
 
@@ -174,10 +199,31 @@
     def line_target(k):
         return {"seq": on_line(k) * PLANE + spot}
 
-    def plane_target(k):
-        return {"seq": line * PLANE + on_plane(k)}
+    def plane_target(where):
+        return {"seq": line * PLANE + where}
 
     sibling = {"geo": 1 - core}
+
+    def to_line(whole, sem):
+        block = whole.at[line, spot, :, mine]
+        for k in range(1, lines):
+            send(block, block, sem.at[line, spot], line_target(k))
+
+    def to_plane(whole, sem, at):
+        block = whole.at[at, spot, :, mine]
+        send(block, block, sem.at[at, spot], plane_target(near))
+        send(block, block, sem.at[at, spot], plane_target(far))
+
+    def to_cross(whole, sem, at):
+        block = whole.at[at, near, :, mine]
+        send(block, block, sem.at[at, near], plane_target(far))
+
+    def to_sibling(whole, sem, at, where):
+        block = whole.at[at, where, :, mine]
+        send(block, block, sem.at[at, where], sibling)
+
+    def weight_arrived(whole, sem, at, where):
+        arrived(whole.at[at, where, :, mine], sem.at[at, where])
 
     for k in range(1, lines):
         block = na_all.at[line, spot]
@@ -186,39 +232,26 @@
         to = (me + k) % count
         start = pl.multiple_of(width + to * LANES, LANES)
         send(w_qkv_ref.at[:, pl.ds(start, LANES)], wkv.at[me], a2a_sem.at[me], {"seq": to})
-
-    def to_line(whole, sem):
-        block = whole.at[line, spot, :, mine]
-        for k in range(1, lines):
-            send(block, block, sem.at[line, spot], line_target(k))
-
-    def to_plane(whole, sem, at):
-        block = whole.at[at, spot, :, mine]
-        for k in range(1, PLANE):
-            send(block, block, sem.at[at, spot], plane_target(k))
-
-    def to_sibling(whole, sem, at, where):
-        block = whole.at[at, where, :, mine]
-        send(block, block, sem.at[at, where], sibling)
-
     to_line(wq_all, wq_sem)
     to_plane(wq_all, wq_sem, line)
-    to_line(wo_all, wo_sem)
-
+
+    for k in range(1, lines):
+        arrived(na_all.at[on_line(k), spot], na_sem.at[on_line(k)])
+    for k in range(1, PLANE):
+        block = na_all.at[:, spot]
+        send(block, block, na_sem.at[lines + spot], plane_target(on_plane(k)))
+
+    loads[5].wait()
     values = queries_ref[...].astype(jnp.float32)
     scale = lax.rsqrt(jnp.mean(values * values, axis=-1, keepdims=True) + 1e-05)
     norm_ref[pl.ds(0, rows), :] = (values * scale * gain).astype(jnp.bfloat16)
 
     for k in range(1, lines):
-        arrived(na_all.at[on_line(k), spot], na_sem.at[on_line(k)])
-    for k in range(1, PLANE):
-        block = na_all.at[:, spot]
-        send(block, block, na_sem.at[lines + spot], plane_target(k))
-    for k in range(1, lines):
         at = on_line(k)
-        arrived(wq_all.at[at, spot, :, mine], wq_sem.at[at, spot])
+        weight_arrived(wq_all, wq_sem, at, spot)
         to_plane(wq_all, wq_sem, at)
         to_sibling(wq_all, wq_sib_sem, at, spot)
+    to_line(wo_all, wo_sem)
 
     for k in range(1, PLANE):
         arrived(na_all.at[:, on_plane(k)], na_sem.at[lines + on_plane(k)])
@@ -236,24 +269,29 @@
     for k in range(1, lines):
         block = kv_all.at[line, spot]
         send(block, block, kv_sem.at[line], line_target(k))
+    for k in range(lines):
+        weight_arrived(wq_all, wq_sem, on_line(k), near)
+        to_cross(wq_all, wq_sem, on_line(k))
+        to_sibling(wq_all, wq_sib_sem, on_line(k), near)
+    for k in range(1, lines):
+        arrived(kv_all.at[on_line(k), spot], kv_sem.at[on_line(k)])
+    block = kv_all.at[:, spot]
+    send(block, block, kv_sem.at[lines + spot], plane_target(near))
+    send(block, block, kv_sem.at[lines + spot], plane_target(far))
     to_plane(wo_all, wo_sem, line)
     for k in range(1, lines):
-        arrived(kv_all.at[on_line(k), spot], kv_sem.at[on_line(k)])
-    for k in range(1, PLANE):
-        block = kv_all.at[:, spot]
-        send(block, block, kv_sem.at[lines + spot], plane_target(k))
-    for k in range(1, lines):
         at = on_line(k)
-        arrived(wo_all.at[at, spot, :, mine], wo_sem.at[at, spot])
+        weight_arrived(wo_all, wo_sem, at, spot)
         to_plane(wo_all, wo_sem, at)
         to_sibling(wo_all, wo_sib_sem, at, spot)
-
-    def rest_to_sibling(whole, sem, sib_sem):
-        for j in range(lines):
-            for k in range(1, PLANE):
-                at, where = on_line(j), on_plane(k)
-                arrived(whole.at[at, where, :, mine], sem.at[at, where])
-                to_sibling(whole, sib_sem, at, where)
+    arrived(kv_all.at[:, near], kv_sem.at[lines + near])
+    block = kv_all.at[:, near]
+    send(block, block, kv_sem.at[lines + near], plane_target(far))
+
+    for where in (far, cross):
+        for k in range(lines):
+            weight_arrived(wq_all, wq_sem, on_line(k), where)
+            to_sibling(wq_all, wq_sib_sem, on_line(k), where)
 
     def from_sibling(whole, sib_sem):
         for j in range(lines):
@@ -262,9 +300,23 @@
                     at, where = on_line(j), on_plane(k)
                     arrived(whole.at[at, where, :, other], sib_sem.at[at, where])
 
-    rest_to_sibling(wq_all, wq_sem, wq_sib_sem)
     from_sibling(wq_all, wq_sib_sem)
     step = 2 * LANES
+
+    later = [(on_line(k), near) for k in range(lines)]
+    later += [(on_line(k), far) for k in range(lines)]
+    later += [(on_line(k), cross) for k in range(lines)]
+
+    def pass_on(steps):
+        for _ in range(steps):
+            if later:
+                first = len(later) > 2 * lines
+                at, where = later.pop(0)
+                weight_arrived(wo_all, wo_sem, at, where)
+                if first:
+                    to_cross(wo_all, wo_sem, at)
+                to_sibling(wo_all, wo_sib_sem, at, where)
+
     for j in range(width // step):
         columns = pl.ds(j * step, step)
         block = wq_all[:, :, :, columns].reshape(width, step)
@@ -272,8 +324,8 @@
             norm_ref[...], block, preferred_element_type=jnp.float32
         ).astype(jnp.bfloat16)
 
-    for k in range(1, PLANE):
-        arrived(kv_all.at[:, on_plane(k)], kv_sem.at[lines + on_plane(k)])
+    arrived(kv_all.at[:, far], kv_sem.at[lines + far])
+    arrived(kv_all.at[:, cross], kv_sem.at[lines + cross])
 
     head = width // HEADS
     factor = head ** (-0.5)
@@ -288,6 +340,7 @@
 
     pairs = HEADS // 2
     for pair in range(pairs):
+        pass_on(2)
         columns = pl.ds(pair * LANES, LANES)
         scores = lax.dot_general(
             q_ref[:, columns],
@@ -308,7 +361,7 @@
         total = jnp.where(upper_ctx, totals[1], totals[0])
         ctx_ref[:, columns] = (mixed / total).astype(jnp.bfloat16)
 
-    rest_to_sibling(wo_all, wo_sem, wo_sib_sem)
+    pass_on(len(later))
     from_sibling(wo_all, wo_sib_sem)
     for j in range(width // step):
         columns = pl.ds(j * step, step)
@@ -332,15 +385,19 @@
     bf16 = jnp.bfloat16
     copies = 2 * (lines - 1 + PLANE - 1) + count - 1
     copies += 2 * (lines - 1 + lines * (PLANE - 1) + count - 1)
+    hbm = pl.BlockSpec(memory_space=pltpu.HBM)
     return pl.pallas_call(
         functools.partial(kernel, lines),
         out_shape=(
             jax.ShapeDtypeStruct((anchors, width), bf16),
             jax.ShapeDtypeStruct((rows, width), bf16),
         ),
-        in_specs=[pl.BlockSpec(memory_space=pltpu.SMEM)] + [vmem] * 5,
+        in_specs=[pl.BlockSpec(memory_space=pltpu.SMEM)] + [hbm] * 5,
         out_specs=(vmem, vmem),
         scratch_shapes=[
+            pltpu.VMEM(cells.shape, bf16),
+            pltpu.VMEM(queries.shape, bf16),
+            pltpu.VMEM((1, width), jnp.float32),
             pltpu.VMEM((padded, width), bf16),
             pltpu.VMEM((padded, width), bf16),
             pltpu.VMEM((padded, width), bf16),
@@ -349,6 +406,7 @@
             pltpu.VMEM((*grid, count * anchors, LANES), bf16),
             pltpu.VMEM((*grid, depth, width), bf16),
             pltpu.VMEM((*grid, depth, width), bf16),
+            pltpu.SemaphoreType.DMA((6,)),
             pltpu.SemaphoreType.DMA((copies,)),
             pltpu.SemaphoreType.DMA((lines + PLANE,)),
             pltpu.SemaphoreType.DMA((count,)),
@@ -359,7 +417,7 @@
             pltpu.SemaphoreType.DMA(grid),
         ],
         compiler_params=pltpu.CompilerParams(
-            collective_id=0, has_side_effects=True, vmem_limit_bytes=40 * 1024 * 1024
+            collective_id=0, has_side_effects=True, vmem_limit_bytes=60 * 1024 * 1024
         ),
         cost_estimate=pl.CostEstimate(
             flops=4 * padded * width * width, bytes_accessed=4 * width * width, transcendentals=0

time: 59.9 us -> 53.6 us (0.89)
  the two profiles are of different devices: /device:TPU:9 before, /device:TPU:25 now
where the time goes in v2:
time: 53.6 us; the launch traced here: 53.3 us
  Pallas kernels  49.5 us (92%)
  local copies, waits for them, and re-layouts  3.19 us (6%)
  between operations  0.64 us (1%)
    pallas_call x1, Pallas kernels, fused(): pl.pallas_call(functools.partial(kernel, lines), out_shape=(jax.ShapeDtyp...  49.5 us
    unnamed x2, local copies, waits for them, and re-layouts  3.19 us

profile of v2, /device:TPU:25, one launch (start us, length us, event | category | flops | bytes accessed | tf_op | source)
XLA Modules:
  0.0 53.3 jit_solution(15223589641999109567)
XLA Ops:
  0.6 49.5 %shard_map.77 = (bf16[8,1024]{1,0:T(8,128)(2,1)}, bf16[256,1024]{1,0:T(8,128)(2,1)}) custom-call(s32[8]{0:T(128)} %index_ref.1, bf16[256,1024]{1,0:T(8,128)(2,1)} %cells_hbm.1, bf16[256,1024]{1,0:T(8,128)(2,1)} %queries_hbm.1, f32[1,1024]{1,0:T(1,128)} %bitcast.1, bf16[64,3072]{1,0:T(8,128)(2,1)} %w_qkv_ref.1, bf16[64,1024]{1,0:T(8,128)(2,1)} %w_out_ref.1), custom_call_target="tpu_custom_call" | custom-call | flops 1140850688 | bytes 4194304 | tf_op jit(solution)/shard_map/pallas_call | solution.py:389
  50.2 1.3 %copy.10 = bf16[8,1024]{1,0:T(8,128)(2,1)} copy(bf16[8,1024]{1,0:T(8,128)(2,1)} %get-tuple-element.4) | data formatting | bytes 32768
  51.5 1.9 %copy.11 = bf16[256,1024]{1,0:T(8,128)(2,1)} copy(bf16[256,1024]{1,0:T(8,128)(2,1)} %get-tuple-element.5) | data formatting | bytes 1048576

commit v3 on v2

--- a/solution.py
+++ b/solution.py
@@ -129,12 +129,15 @@
     pl.semaphore_signal(barrier, inc=1, device_id={"geo": 1 - core}, device_id_type=MESH)
 
     start = pl.multiple_of(width + me * LANES, LANES)
+    share = w_qkv_ref.shape[0] // 2
+    part = pl.ds(pl.multiple_of(core * share, share), share)
+    rest = pl.ds(pl.multiple_of((1 - core) * share, share), share)
     loads = []
     for source, target in (
         (cells_hbm, cells_ref),
         (gain_hbm, gain_ref),
         (w_qkv_ref.at[:, pl.ds(0, width)], wq_all.at[line, spot]),
-        (w_qkv_ref.at[:, pl.ds(start, LANES)], wkv.at[me]),
+        (w_qkv_ref.at[part, pl.ds(start, LANES)], wkv.at[me, part]),
         (w_out_ref, wo_all.at[line, spot]),
         (queries_hbm, queries_ref),
     ):
@@ -231,33 +234,29 @@
     for k in range(1, count):
         to = (me + k) % count
         start = pl.multiple_of(width + to * LANES, LANES)
-        send(w_qkv_ref.at[:, pl.ds(start, LANES)], wkv.at[me], a2a_sem.at[me], {"seq": to})
-    to_line(wq_all, wq_sem)
-    to_plane(wq_all, wq_sem, line)
+        block = w_qkv_ref.at[part, pl.ds(start, LANES)]
+        send(block, wkv.at[me, part], a2a_sem.at[me], {"seq": to})
 
     for k in range(1, lines):
         arrived(na_all.at[on_line(k), spot], na_sem.at[on_line(k)])
     for k in range(1, PLANE):
         block = na_all.at[:, spot]
         send(block, block, na_sem.at[lines + spot], plane_target(on_plane(k)))
+    to_line(wq_all, wq_sem)
+    to_plane(wq_all, wq_sem, line)
 
     loads[5].wait()
     values = queries_ref[...].astype(jnp.float32)
     scale = lax.rsqrt(jnp.mean(values * values, axis=-1, keepdims=True) + 1e-05)
     norm_ref[pl.ds(0, rows), :] = (values * scale * gain).astype(jnp.bfloat16)
 
-    for k in range(1, lines):
-        at = on_line(k)
-        weight_arrived(wq_all, wq_sem, at, spot)
-        to_plane(wq_all, wq_sem, at)
-        to_sibling(wq_all, wq_sib_sem, at, spot)
-    to_line(wo_all, wo_sem)
-
+    for k in range(1, count):
+        source = (me + k) % count
+        arrived(wkv.at[source, part], a2a_sem.at[source])
+    send(wkv.at[:, part], wkv.at[:, part], a2a_sem.at[count], sibling)
     for k in range(1, PLANE):
         arrived(na_all.at[:, on_plane(k)], na_sem.at[lines + on_plane(k)])
-    for k in range(1, count):
-        source = (me + k) % count
-        arrived(wkv.at[source], a2a_sem.at[source])
+    arrived(wkv.at[:, rest], a2a_sem.at[count])
     packed = na_all[...].reshape(count * 2 * anchors, half)
     slab = wkv[...].reshape(width, LANES)
     low = jnp.dot(packed, slab[:half], preferred_element_type=jnp.float32)
@@ -269,6 +268,12 @@
     for k in range(1, lines):
         block = kv_all.at[line, spot]
         send(block, block, kv_sem.at[line], line_target(k))
+    for k in range(1, lines):
+        at = on_line(k)
+        weight_arrived(wq_all, wq_sem, at, spot)
+        to_plane(wq_all, wq_sem, at)
+        to_sibling(wq_all, wq_sib_sem, at, spot)
+    to_line(wo_all, wo_sem)
     for k in range(lines):
         weight_arrived(wq_all, wq_sem, on_line(k), near)
         to_cross(wq_all, wq_sem, on_line(k))
@@ -383,7 +388,7 @@
     vmem = pl.BlockSpec(memory_space=pltpu.VMEM)
     grid = (lines, PLANE)
     bf16 = jnp.bfloat16
-    copies = 2 * (lines - 1 + PLANE - 1) + count - 1
+    copies = 2 * (lines - 1 + PLANE - 1) + count
     copies += 2 * (lines - 1 + lines * (PLANE - 1) + count - 1)
     hbm = pl.BlockSpec(memory_space=pltpu.HBM)
     return pl.pallas_call(
@@ -409,7 +414,7 @@
             pltpu.SemaphoreType.DMA((6,)),
             pltpu.SemaphoreType.DMA((copies,)),
             pltpu.SemaphoreType.DMA((lines + PLANE,)),
-            pltpu.SemaphoreType.DMA((count,)),
+            pltpu.SemaphoreType.DMA((count + 1,)),
             pltpu.SemaphoreType.DMA((lines + PLANE,)),
             pltpu.SemaphoreType.DMA(grid),
             pltpu.SemaphoreType.DMA(grid),
@@ -437,6 +442,7 @@
             and count * LANES == 2 * width
             and HEADS * LANES == 2 * width
             and count * anchor_index.shape[0] == LANES
+            and w_qkv.shape[0] % 32 == 0
         )
         if tiles:
             return fused(count // PLANE, *args)

time: 53.6 us -> 50.9 us (0.950)
  Pallas kernels: 49.5 us -> 46.8 us
    pallas_call x1, Pallas kernels: 49.5 us -> 46.8 us  [fused(): pl.pallas_call(functools.partial(kernel, lines), out_shape=(jax.ShapeDtyp...]
where the time goes in v3:
time: 50.9 us; the launch traced here: 50.7 us
  Pallas kernels  46.8 us (92%)
  local copies, waits for them, and re-layouts  3.19 us (6%)
  between operations  0.64 us (1%)
    pallas_call x1, Pallas kernels, fused(): pl.pallas_call(functools.partial(kernel, lines), out_shape=(jax.ShapeDtyp...  46.8 us
    unnamed x2, local copies, waits for them, and re-layouts  3.19 us

profile of v3, /device:TPU:25, one launch (start us, length us, event | category | flops | bytes accessed | tf_op | source)
XLA Modules:
  0.0 50.7 jit_solution(17347217360404017206)
XLA Ops:
  0.6 46.8 %shard_map.77 = (bf16[8,1024]{1,0:T(8,128)(2,1)}, bf16[256,1024]{1,0:T(8,128)(2,1)}) custom-call(s32[8]{0:T(128)} %index_ref.1, bf16[256,1024]{1,0:T(8,128)(2,1)} %cells_hbm.1, bf16[256,1024]{1,0:T(8,128)(2,1)} %queries_hbm.1, f32[1,1024]{1,0:T(1,128)} %bitcast.1, bf16[64,3072]{1,0:T(8,128)(2,1)} %w_qkv_ref.1, bf16[64,1024]{1,0:T(8,128)(2,1)} %w_out_ref.1), custom_call_target="tpu_custom_call" | custom-call | flops 1140850688 | bytes 4194304 | tf_op jit(solution)/shard_map/pallas_call | solution.py:394
  47.5 1.3 %copy.10 = bf16[8,1024]{1,0:T(8,128)(2,1)} copy(bf16[8,1024]{1,0:T(8,128)(2,1)} %get-tuple-element.4) | data formatting | bytes 32768
  48.8 1.9 %copy.11 = bf16[256,1024]{1,0:T(8,128)(2,1)} copy(bf16[256,1024]{1,0:T(8,128)(2,1)} %get-tuple-element.5) | data formatting | bytes 1048576

commit v4 on v3

--- a/solution.py
+++ b/solution.py
@@ -254,6 +254,11 @@
         source = (me + k) % count
         arrived(wkv.at[source, part], a2a_sem.at[source])
     send(wkv.at[:, part], wkv.at[:, part], a2a_sem.at[count], sibling)
+    for k in range(1, lines):
+        at = on_line(k)
+        weight_arrived(wq_all, wq_sem, at, spot)
+        to_plane(wq_all, wq_sem, at)
+        to_sibling(wq_all, wq_sib_sem, at, spot)
     for k in range(1, PLANE):
         arrived(na_all.at[:, on_plane(k)], na_sem.at[lines + on_plane(k)])
     arrived(wkv.at[:, rest], a2a_sem.at[count])
@@ -268,11 +273,6 @@
     for k in range(1, lines):
         block = kv_all.at[line, spot]
         send(block, block, kv_sem.at[line], line_target(k))
-    for k in range(1, lines):
-        at = on_line(k)
-        weight_arrived(wq_all, wq_sem, at, spot)
-        to_plane(wq_all, wq_sem, at)
-        to_sibling(wq_all, wq_sib_sem, at, spot)
     to_line(wo_all, wo_sem)
     for k in range(lines):
         weight_arrived(wq_all, wq_sem, on_line(k), near)

time: 50.9 us -> 48.7 us (0.957); the launches traced: 50.7 us -> 47.9 us
  Pallas kernels: 46.8 us -> 44 us
    pallas_call x1, Pallas kernels: 46.8 us -> 44 us  [fused(): pl.pallas_call(functools.partial(kernel, lines), out_shape=(jax.ShapeDtyp...]
where the time goes in v4:
time: 48.7 us; the launch traced here: 47.9 us
  Pallas kernels  44 us (90%)
  local copies, waits for them, and re-layouts  3.19 us (7%)
  between operations  0.64 us (1%)
    pallas_call x1, Pallas kernels, fused(): pl.pallas_call(functools.partial(kernel, lines), out_shape=(jax.ShapeDtyp...  44 us
    unnamed x2, local copies, waits for them, and re-layouts  3.19 us

profile of v4, /device:TPU:25, one launch (start us, length us, event | category | flops | bytes accessed | tf_op | source)
XLA Modules:
  0.0 47.9 jit_solution(16093906984380978797)
XLA Ops:
  0.6 44.0 %shard_map.77 = (bf16[8,1024]{1,0:T(8,128)(2,1)}, bf16[256,1024]{1,0:T(8,128)(2,1)}) custom-call(s32[8]{0:T(128)} %index_ref.1, bf16[256,1024]{1,0:T(8,128)(2,1)} %cells_hbm.1, bf16[256,1024]{1,0:T(8,128)(2,1)} %queries_hbm.1, f32[1,1024]{1,0:T(1,128)} %bitcast.1, bf16[64,3072]{1,0:T(8,128)(2,1)} %w_qkv_ref.1, bf16[64,1024]{1,0:T(8,128)(2,1)} %w_out_ref.1), custom_call_target="tpu_custom_call" | custom-call | flops 1140850688 | bytes 4194304 | tf_op jit(solution)/shard_map/pallas_call | solution.py:394
  44.7 1.3 %copy.10 = bf16[8,1024]{1,0:T(8,128)(2,1)} copy(bf16[8,1024]{1,0:T(8,128)(2,1)} %get-tuple-element.4) | data formatting | bytes 32768
  46.0 1.9 %copy.11 = bf16[256,1024]{1,0:T(8,128)(2,1)} copy(bf16[256,1024]{1,0:T(8,128)(2,1)} %get-tuple-element.5) | data formatting | bytes 1048576
